TPU v7x, 256 devices: a whole 4x4x8 slice. The times are simulated.
256 devices in a mesh: row: 8 (over x_lo, y), col: 32 (over z, x_hi, core).
Axes of the slice: x: 4 (x_hi: 2, x_lo: 2; x = x_hi * 2 + x_lo), y: 4, z: 8, core: 2. Of those that a mesh axis runs over, the one named last changes fastest.
Arguments:
- markov: bfloat16 [8192, 8192], P('row', 'col'), may hold values from 0.049804688 to 1
- input_tiles: int32 [64, 64], P('row', 'col'), may hold values from 0 to 1, as said below
- keep_tiles: int32 [64, 64], P('row', 'col'), may hold values from 0 to 1, as said below
Outputs:
- clustered: bfloat16 [8192, 8192], P('row', 'col')
Inputs may be any that keep to these rules, and one draw needn't show every extreme that they name: `input_tiles`: entries are 0 or 1; every diagonal tile is 1. Each device's block of 8 x 2 tiles holds at most 8 ones, and some block holds exactly 8. `keep_tiles`: entries are 0 or 1; every diagonal tile is 1.
All inputs are finite; a program needn't handle non-finite values.
Results may differ from a plain program's by a relative error of at most 0.001.
Values may be sent and summed in bfloat16 or wider, within the bound.
A program may use at most 128 MiB of HBM per device.

v0:
```python
import jax
import jax.numpy as jnp
from jax import lax
from jax.sharding import PartitionSpec as P


def spread(pattern, tile_width):
    return jnp.repeat(jnp.repeat(pattern, tile_width, axis=0), tile_width, axis=1)


def body(markov, input_tiles, keep_tiles):
    tile_width = markov.shape[0] // input_tiles.shape[0]
    order_all = markov.shape[1] * lax.axis_size("col")
    masked = markov * spread(input_tiles, tile_width).astype(jnp.bfloat16)
    right_whole = lax.all_gather(masked, "row", axis=0, tiled=True)
    square = jnp.dot(
        lax.all_gather(masked, "col", axis=1, tiled=True),
        right_whole,
        preferred_element_type=jnp.float32,
    )
    inflated = square * square * spread(keep_tiles, tile_width).astype(jnp.float32)
    colsum = lax.psum(jnp.sum(inflated, axis=0), "row")
    return (jnp.float32(order_all) * inflated / colsum[None, :]).astype(jnp.bfloat16)


def solution(mesh):
    in_specs = (P("row", "col"), P("row", "col"), P("row", "col"))
    out_specs = P("row", "col")
    return jax.shard_map(body, mesh=mesh, in_specs=in_specs, out_specs=out_specs, check_vma=False)
```

profile of v0, /device:TPU:1, one launch (start us, length us, event | category | flops | bytes accessed | tf_op | source)
XLA Modules:
  0.0 259.2 jit_solution(11813286942243285228)
XLA Ops:
  6.5 0.0 all-gather.5.cloned.1.call-start
  6.5 0.7 convert_element_type.25
  7.2 0.1 copy.4
  7.4 2.9 %broadcast_in_dim.14 = bf16[1024,2,128]{2,1,0:T(2,128)(2,1)S(1)} broadcast(bf16[1024,2]{1,0:T(8,128)(2,1)S(1)} %bitcast.12), dimensions={0,1} | broadcast | bytes 528384 | tf_op jit(solution)/shard_map/broadcast_in_dim | solution.py:8
  10.3 1.9 bitcast_multiply_fusion
  12.2 0.0 all-gather.5.cloned.1.call-update
  12.2 0.0 all-gather.3.cloned.1.call-start
  12.3 0.7 all-gather.3.cloned.1.call-update
  13.0 0.7 convert_element_type.28
  13.7 0.1 copy.5
  13.8 57.6 %all-gather.5.cloned.1.call-done = bf16[8192,256]{1,0:T(8,128)(2,1)} async-done(((bf16[1024,256]{1,0:T(8,128)(2,1)}), bf16[8192,256]{1,0:T(8,128)(2,1)}) %all-gather.5.cloned.1.call-update) | async-done | bytes 4194320 | tf_op jit(solution)/shard_map/all_gather | solution.py:15
  71.3 154.5 %all-gather.3.cloned.1.call-done = bf16[1024,8192]{1,0:T(8,128)(2,1)} async-done(((bf16[1024,256]{1,0:T(8,128)(2,1)}), bf16[1024,8192]{1,0:T(8,128)(2,1)}) %all-gather.3.cloned.1.call-update) | async-done | bytes 16777232 | tf_op jit(solution)/shard_map/all_gather | solution.py:17
  225.9 1.2 broadcast_in_dim.16
  227.1 9.3 %fusion.1 = (f32[256]{0:T(256)S(1)}, f32[1024,256]{1,0:T(8,128)S(1)}) fusion(f32[128,8,2,128]{3,2,1,0:T(2,128)S(1)} %bitcast.13, bf16[1024,8192]{1,0:T(8,128)(2,1)} %all-gather.3.cloned.1.call-done, bf16[8192,256]{1,0:T(8,128)(2,1)} %all-gather.5.cloned.1.call-done), kind=kOutput, calls=%fused_computation.4 | convolution fusion | flops 4295753728 | bytes 23069696 | tf_op jit(solution)/shard_map/dot_general | solution.py:16
  236.5 14.9 %psum.7 = f32[256]{0:T(256)S(1)} all-reduce(f32[256]{0:T(256)S(1)} %get-tuple-element.5), channel_id=1, replica_groups=mesh['row'=8,'col'=32] {'row'}, use_global_device_ids=true, to_apply=%region_1.0 | all-reduce | flops 256 | bytes 2048 | tf_op jit(solution)/shard_map/psum | solution.py:22
  251.4 0.9 divide_convert_fusion
  (2 shorter events, 0.1 us)
Async XLA Ops:
  6.5 64.8 %all-gather.5.cloned.1.call-start = ((), (), s32[]{:S(2)}) async-start(), calls=%async_computation.1 | async-start | bytes 4718592 | tf_op jit(solution)/shard_map/all_gather | solution.py:15
  12.2 213.6 %all-gather.3.cloned.1.call-start = ((), (), s32[]{:S(2)}) async-start(), calls=%async_computation | async-start | bytes 17301504 | tf_op jit(solution)/shard_map/all_gather | solution.py:17
Sparse Core Ops, SparseCore 0:
  12.4 58.9 all-gather.4
  73.9 151.9 all-gather.2
where the time goes:
time: 262 us; the launch traced here: 259 us
  waiting for transfers between devices  213 us (81%)
  blocking collectives  14.9 us (6%)
  between operations  13.4 us (5%)
  matrix products  9.34 us (4%)
  local copies, waits for them, and re-layouts  4.43 us (2%)
  other arithmetic  4.16 us (2%)
    all_gather x1, waiting for transfers between devices, body(): lax.all_gather(masked, 'col', axis=1, tiled=True)  155 us
    all_gather x1, waiting for transfers between devices, body(): right_whole = lax.all_gather(masked, 'row', axis=0, tiled=True)  57.6 us
    psum x1, blocking collectives, body(): colsum = lax.psum(jnp.sum(inflated, axis=0), 'row')  14.9 us
    dot_general x1, matrix products, body(): jnp.dot(lax.all_gather(masked, 'col', axis=1, tiled=True), right_whole, p...  9.34 us
  transfers between devices with their start and end apart: 2, of which 2 were waited for; matrix products, arithmetic and copies ran while one was open for 0% of the time, Pallas kernels for 0%

commit v1 on v0

v1 whole, which is shorter than its diff:
```python
import jax
import jax.numpy as jnp
from jax import lax
from jax.experimental import pallas as pl
from jax.experimental.pallas import tpu as pltpu
from jax.sharding import PartitionSpec as P

MESH = pl.DeviceIdType.MESH
T = 128
RT, CT = 8, 2
SLOTS = 8
PT = 4
NZ, NY, NROW = 8, 4, 8
BLOCK = RT * T
COPIES = 96


def kernel(mk, it, kt, out, g0, g1, g2, g3, g4, g5, g6, g7, col, rhs, lhs, acc, cs, tabs, ctabs, ssem, rsem):
    groups = (g0, g1, g2, g3, g4, g5, g6, g7)
    me_row, me_col = lax.axis_index("row"), lax.axis_index("col")
    xlo, y = me_row // NY, me_row % NY
    z, xh, core = me_col // 4, (me_col // 2) % 2, me_col % 2

    def zdev(d):
        return (me_row, ((z + d + NZ) % NZ) * 4 + xh * 2 + core)

    def ydev(d):
        return (xlo * NY + (y + d + NY) % NY, me_col)

    xdev = (me_row, z * 4 + (1 - xh) * 2 + core)
    xldev = ((1 - xlo) * NY + y, me_col)
    cdev = (me_row, z * 4 + xh * 2 + (1 - core))
    peers = [((me_row + j) % NROW, me_col) for j in range(1, NROW)]

    barrier = pltpu.get_barrier_semaphore()
    for dev in [zdev(1), zdev(-1), xdev, cdev] + peers:
        pl.semaphore_signal(barrier, inc=1, device_id=dev, device_id_type=MESH)

    count = [0]
    started = []

    def send(src, dst, dev):
        k = count[0]
        count[0] += 1
        copy = pltpu.make_async_remote_copy(
            src_ref=src, dst_ref=dst, send_sem=ssem.at[k], recv_sem=rsem.at[k], device_id=dev, device_id_type=MESH
        )
        copy.start()
        started.append(copy)
        return copy

    def drain():
        for copy in started:
            copy.wait_send()
        started.clear()

    e0, e1 = core * 2 + xh, core * 2 + (1 - xh)
    front, back, whole = pl.ds(0, PT), pl.ds(PT, SLOTS - PT), pl.ds(0, SLOTS)

    seen = jnp.int32(0)
    place = [(jnp.int32(0), jnp.int32(0))] * SLOTS
    for p in range(RT * CT):
        there = it[p // CT, p % CT] > 0
        slot = jnp.where(there, seen, SLOTS)
        tabs[core * 16 + xh, p] = slot
        ctabs[me_row, p] = slot
        for s in range(min(p + 1, SLOTS)):
            i, k = place[s]
            place[s] = (jnp.where(slot == s, p // CT, i), jnp.where(slot == s, p % CT, k))
        seen = seen + there.astype(jnp.int32)
    for s in range(SLOTS):
        i, k = place[s]
        tile = jnp.where(k == 0, mk[i, :, :T], mk[i, :, T:])
        g0[e0, s] = tile
        col[me_row, s] = tile

    pl.semaphore_wait(barrier, 4 + len(peers))

    px = send(g0.at[e0, front], g0.at[e0, front], xdev)
    tx = send(tabs.at[pl.ds(core * 16 + xh, 1)], tabs.at[pl.ds(core * 16 + xh, 1)], xdev)
    up = {0: groups[0], 1: groups[1], 2: groups[2], 3: groups[3], 4: groups[4]}
    down = {0: groups[0], 1: groups[5], 2: groups[6], 3: groups[7], 4: groups[4]}
    half_f, half_b = PT // 2, (SLOTS - PT) // 2

    def ring(e, lo, n, d):
        if d < 4:
            a = b = pl.ds(lo, n)
        else:
            a, b = pl.ds(lo, n // 2), pl.ds(lo + n // 2, n - n // 2)
        return (
            send(up[d - 1].at[e, a], up[d].at[e, a], zdev(1)),
            send(down[d - 1].at[e, b], down[d].at[e, b], zdev(-1)),
        )

    def arrived(copies):
        for copy in copies:
            copy.wait_recv()

    A, B, C = {}, {}, {}
    Q = {}
    K = {}

    def cross(rel):
        Q[rel] = send(groups[rel].at[e0, back], groups[rel].at[e0, back], xdev)

    def hand(rel):
        src = groups[rel].at[pl.ds(core * 2, 2), whole]
        K[rel] = send(src, src, cdev)

    A[1] = ring(e0, PT, SLOTS - PT, 1)
    xl = send(col.at[me_row, whole], col.at[me_row, whole], xldev)
    y1 = [send(col.at[me_row, whole], col.at[me_row, whole], ydev(d)) for d in (1, -1)]
    B[1] = ring(e0, 0, PT, 1)
    cross(0)
    ct = [send(ctabs.at[pl.ds(me_row, 1)], ctabs.at[pl.ds(me_row, 1)], dev) for dev in peers]

    zero = jnp.zeros((T, T), jnp.bfloat16)
    for g in groups:
        for e in range(4):
            g[e, SLOTS] = zero
    for b in range(NROW):
        col[b, SLOTS] = zero

    def tab(rel):
        return tabs.at[pl.ds(core * 16 + rel * 2, 2)]

    tx.wait_recv()
    tu = send(tab(0), tab(1), zdev(1))
    td = send(tab(0), tab(5), zdev(-1))

    px.wait_recv()
    C[1] = ring(e1, 0, PT, 1)
    arrived(A[1])
    A[2] = ring(e0, PT, SLOTS - PT, 2)
    cross(1)
    cross(5)
    arrived((tu, td))
    tu = send(tab(1), tab(2), zdev(1))
    td = send(tab(5), tab(6), zdev(-1))

    xl.wait_recv()
    other = (1 - xlo) * NY + y
    y1x = [send(col.at[other, whole], col.at[other, whole], ydev(d)) for d in (1, -1)]
    arrived(B[1])
    B[2] = ring(e0, 0, PT, 2)
    arrived(y1)
    lo, hi = pl.ds(0, SLOTS // 2), pl.ds(SLOTS // 2, SLOTS // 2)

    def second(x):
        below, above = x * NY + (y + NY - 1) % NY, x * NY + (y + 1) % NY
        return [
            send(col.at[below, lo], col.at[below, lo], ydev(1)),
            send(col.at[above, hi], col.at[above, hi], ydev(-1)),
        ]

    y2 = second(xlo)
    Q[0].wait_recv()
    hand(0)
    arrived((tu, td))
    tu = send(tab(2), tab(3), zdev(1))
    td = send(tab(6), tab(7), zdev(-1))
    arrived(A[2])
    A[3] = ring(e0, PT, SLOTS - PT, 3)
    cross(2)
    cross(6)
    arrived(C[1])
    C[2] = ring(e1, 0, PT, 2)
    arrived((tu, td))
    tu = send(tab(3), tab(4), zdev(1))
    arrived(B[2])
    B[3] = ring(e0, 0, PT, 3)
    arrived(y1x)
    y2x = second(1 - xlo)
    tu.wait_recv()
    mine = tabs.at[pl.ds(core * 16, 16)]
    tc = send(mine, mine, cdev)
    arrived(ct)
    Q[1].wait_recv()
    hand(1)
    Q[5].wait_recv()
    hand(5)
    arrived(A[3])
    A[4] = ring(e0, PT, SLOTS - PT, 4)
    cross(3)
    cross(7)
    arrived(y2)
    arrived(y2x)

    def column(b, _):
        def step(i, _):
            for k in range(CT):
                rhs[pl.ds(pl.multiple_of(b * BLOCK + i * T, T), T), k * T : (k + 1) * T] = col[b, ctabs[b, i * CT + k]]
            return 0

        return lax.fori_loop(0, RT, step, 0)

    def multiply(rel, owner, first=False):
        K[rel].wait_recv()
        g = groups[rel]

        def unpack(i, _):
            for c in range(2):
                for h in range(2):
                    for k in range(CT):
                        slot = tabs[c * 16 + rel * 2 + h, i * CT + k]
                        at = h * 512 + c * 256 + k * T
                        lhs[pl.ds(pl.multiple_of(i * T, T), T), at : at + T] = g[c * 2 + h, slot]
            return 0

        lax.fori_loop(0, RT, unpack, 0)

        def dot(m, _):
            rows = pl.ds(pl.multiple_of(m * 256, 256), 256)
            part = jnp.dot(
                lhs[rows, :],
                rhs[pl.ds(pl.multiple_of(owner * BLOCK, BLOCK), BLOCK), :],
                preferred_element_type=jnp.float32,
            )
            acc[rows, :] = part if first else acc[rows, :] + part
            return 0

        lax.fori_loop(0, BLOCK // 256, dot, 0)

    lax.fori_loop(0, NROW, column, 0)
    arrived(C[2])
    C[3] = ring(e1, 0, PT, 3)
    tc.wait_recv()
    multiply(0, z, first=True)
    arrived(B[3])
    B[4] = ring(e0, 0, PT, 4)
    multiply(1, (z + NZ - 1) % NZ)
    Q[2].wait_recv()
    hand(2)
    Q[6].wait_recv()
    hand(6)
    arrived(A[4])
    cross(4)
    arrived(C[3])
    C[4] = ring(e1, 0, PT, 4)
    multiply(5, (z + 1) % NZ)
    multiply(2, (z + NZ - 2) % NZ)
    multiply(6, (z + 2) % NZ)
    Q[3].wait_recv()
    hand(3)
    Q[7].wait_recv()
    hand(7)
    arrived(B[4])
    arrived(C[4])
    multiply(3, (z + NZ - 3) % NZ)
    multiply(7, (z + 3) % NZ)
    Q[4].wait_recv()
    hand(4)
    drain()
    multiply(4, (z + 4) % NZ)

    lane = lax.broadcasted_iota(jnp.int32, (1, CT * T), 1)

    def square(i, total):
        rows = pl.ds(pl.multiple_of(i * T, T), T)
        keep = jnp.where(lane < T, kt[i, 0], kt[i, 1]).astype(jnp.float32)
        v = acc[rows, :]
        v = v * v * keep
        acc[rows, :] = v
        return total + jnp.sum(v.reshape(T // 8, 8, CT * T), axis=0)

    cs[me_row] = lax.fori_loop(0, RT, square, jnp.zeros((8, CT * T), jnp.float32))
    sums = [send(cs.at[me_row], cs.at[me_row], dev) for dev in peers]
    arrived(sums)
    total = jnp.sum(jnp.sum(cs[...], axis=0), axis=0, keepdims=True)
    scale = jnp.float32(NZ * BLOCK) / total

    def finish(i, _):
        rows = pl.ds(pl.multiple_of(i * T, T), T)
        out[rows, :] = (acc[rows, :] * scale).astype(jnp.bfloat16)
        return 0

    lax.fori_loop(0, RT, finish, 0)
    drain()


def body(markov, input_tiles, keep_tiles):
    vmem, smem = pl.BlockSpec(memory_space=pltpu.VMEM), pl.BlockSpec(memory_space=pltpu.SMEM)
    return pl.pallas_call(
        kernel,
        out_shape=jax.ShapeDtypeStruct(markov.shape, jnp.bfloat16),
        in_specs=[vmem, smem, smem],
        out_specs=vmem,
        scratch_shapes=[pltpu.VMEM((4, SLOTS + 1, T, T), jnp.bfloat16)] * 8
        + [
            pltpu.VMEM((NROW, SLOTS + 1, T, T), jnp.bfloat16),
            pltpu.VMEM((NZ * BLOCK, CT * T), jnp.bfloat16),
            pltpu.VMEM((BLOCK, BLOCK), jnp.bfloat16),
            pltpu.VMEM((BLOCK, CT * T), jnp.float32),
            pltpu.VMEM((NROW, 8, CT * T), jnp.float32),
            pltpu.SMEM((32, 128), jnp.int32),
            pltpu.SMEM((NROW, 128), jnp.int32),
            pltpu.SemaphoreType.DMA((COPIES,)),
            pltpu.SemaphoreType.DMA((COPIES,)),
        ],
        compiler_params=pltpu.CompilerParams(
            collective_id=0, has_side_effects=True, vmem_limit_bytes=40 * 2**20
        ),
        name="cluster_step",
    )(markov.reshape(RT, T, CT * T), input_tiles, keep_tiles)


def solution(mesh):
    specs = (P("row", "col"), P("row", "col"), P("row", "col"))
    return jax.shard_map(body, mesh=mesh, in_specs=specs, out_specs=P("row", "col"), check_vma=False)
```

time: 262 us -> 63.8 us (0.24); the launches traced: 259 us -> 63.7 us
  waiting for transfers between devices: 213 us -> 0 us
  Pallas kernels: 0 us -> 60.4 us
  blocking collectives: 14.9 us -> 0 us
  between operations: 13.4 us -> 0.01 us
  matrix products: 9.34 us -> 0 us
  other arithmetic: 4.16 us -> 0 us
    all_gather x2 -> x0, waiting for transfers between devices: 212 us -> none  [the longest x1 155 us: body(): lax.all_gather(masked, 'col', axis=1, tiled=True)]
    pallas_call x0 -> x1, Pallas kernels: none -> 60.4 us  [body(): pl.pallas_call(kernel, out_shape=jax.ShapeDtypeStruct(markov.shape, jnp.b...]
    psum x1 -> x0, blocking collectives: 14.9 us -> none  [body(): colsum = lax.psum(jnp.sum(inflated, axis=0), 'row')]
    dot_general x1 -> x0, matrix products: 9.34 us -> none  [body(): jnp.dot(lax.all_gather(masked, 'col', axis=1, tiled=True), right_whole, p...]
    broadcast_in_dim x4 -> x0, local copies, waits for them, and re-layouts: 4.25 us -> none  [the longest x2 4.17 us: spread(): jnp.repeat(jnp.repeat(pattern, tile_width, axis=0), tile_width, axis=1)]
    unnamed x0 -> x9, local copies, waits for them, and re-layouts: none -> 3.27 us
  transfers between devices with their start and end apart: 2 -> 0, of which waited for: 2 -> 0; matrix products, arithmetic and copies ran while one was open for 0% -> 0% of each run, Pallas kernels for 0% -> 0%
where the time goes in v1:
time: 63.8 us; the launch traced here: 63.7 us
  Pallas kernels  60.4 us (95%)
  local copies, waits for them, and re-layouts  3.27 us (5%)
    pallas_call x1, Pallas kernels, body(): pl.pallas_call(kernel, out_shape=jax.ShapeDtypeStruct(markov.shape, jnp.b...  60.4 us
    unnamed x9, local copies, waits for them, and re-layouts  3.27 us

profile of v1, /device:TPU:1, one launch (start us, length us, event | category | flops | bytes accessed | tf_op | source)
XLA Modules:
  0.0 63.7 jit_solution(3702689017183435573)
XLA Ops:
  0.0 0.0 copy-start.1
  0.0 0.7 %copy-done.1 = s32[8,2]{0,1:T(2,128)S(1)} copy-done((s32[8,2]{0,1:T(2,128)S(1)}, s32[8,2]{0,1:T(2,128)}, u32[]{:S(2)}) %copy-start.1) | copy-done | bytes 88
  0.7 0.0 copy-start.2
  0.7 0.1 copy.4.it
  0.8 0.6 copy-done.2
  1.4 0.1 copy.5.kt
  1.4 0.0 copy-start
  1.4 1.0 %copy-done = bf16[1024,256]{1,0:T(8,128)(2,1)S(1)} copy-done((bf16[1024,256]{1,0:T(8,128)(2,1)S(1)}, bf16[1024,256]{1,0:T(8,128)(2,1)}, u32[]{:S(2)}) %copy-start) | copy-done | bytes 524312
  2.5 60.4 %cluster_step.1 = bf16[1024,256]{1,0:T(8,128)(2,1)S(1)} custom-call(bf16[8,128,256]{2,1,0:T(8,128)(2,1)S(1)} %bitcast.1, s32[8,2]{1,0:T(8,128)S(1)} %copy.4.it, s32[8,2]{1,0:T(8,128)S(1)} %copy.5.kt), custom_call_target="tpu_custom_call" | custom-call | tf_op jit(solution)/shard_map/cluster_step/pallas_call | solution.py:283
  62.9 0.8 %copy.7 = bf16[1024,256]{1,0:T(8,128)(2,1)} copy(bf16[1024,256]{1,0:T(8,128)(2,1)S(1)} %cluster_step.1) | data formatting | bytes 1048576
Async XLA Ops:
  0.0 0.7 %copy-start.1 = (s32[8,2]{0,1:T(2,128)S(1)}, s32[8,2]{0,1:T(2,128)}, u32[]{:S(2)}) copy-start(s32[8,2]{0,1:T(2,128)} %param.4) | copy-start | bytes 196
  0.7 0.7 %copy-start.2 = (s32[8,2]{0,1:T(2,128)S(1)}, s32[8,2]{0,1:T(2,128)}, u32[]{:S(2)}) copy-start(s32[8,2]{0,1:T(2,128)} %param.5) | copy-start | bytes 196
  1.4 1.0 %copy-start = (bf16[1024,256]{1,0:T(8,128)(2,1)S(1)}, bf16[1024,256]{1,0:T(8,128)(2,1)}, u32[]{:S(2)}) copy-start(bf16[1024,256]{1,0:T(8,128)(2,1)} %param.3) | copy-start | bytes 1572868

commit v2 on v0

v2 whole, which is shorter than its diff:
```python
import jax
import jax.numpy as jnp
from jax import lax
from jax.experimental import pallas as pl
from jax.experimental.pallas import tpu as pltpu
from jax.sharding import PartitionSpec as P

MESH = pl.DeviceIdType.MESH
T = 128
RT, CT = 8, 2
SLOTS = 8
HALF = T // 2
PACKED = 2 * SLOTS
FRONT = 9
NZ, NY, NROW = 8, 4, 8
BLOCK = RT * T
WIDTH = CT * T
COPIES = 96


def kernel(
    mk_hbm, it_hbm, kt_hbm, out, own0, own1, own2, own3, own4, far0, far1, far2, far3, far4, c0, cx, cy, cyx, c2, c2x,
    rhs, lhs, acc, cs, mk, it, kt, tabs, ctabs, insem, ssem, rsem,
):
    blocks = ((own0, own1, own2, own3, own4), (far0, far1, far2, far3, far4))
    me_row, me_col = lax.axis_index("row"), lax.axis_index("col")
    xlo, y = me_row // NY, me_row % NY
    z, xh, core = me_col // 4, (me_col // 2) % 2, me_col % 2
    zdevs = [(me_row, ((z + d) % NZ) * 4 + xh * 2 + core) for d in range(1, NZ)]
    up, down = zdevs[0], zdevs[-1]
    yup, ydown = [(xlo * NY + (y + d) % NY, me_col) for d in (1, NY - 1)]
    xdev = (me_row, z * 4 + (1 - xh) * 2 + core)
    xldev = ((1 - xlo) * NY + y, me_col)
    cdev = (me_row, z * 4 + xh * 2 + (1 - core))
    peers = [((me_row + j) % NROW, me_col) for j in range(1, NROW)]

    inputs = [(it_hbm, it), (mk_hbm, mk), (kt_hbm, kt)]
    fetch = [pltpu.make_async_copy(src, dst, insem.at[n]) for n, (src, dst) in enumerate(inputs)]
    for copy in fetch:
        copy.start()
    barrier = pltpu.get_barrier_semaphore()
    for dev in zdevs + [xdev, cdev] + peers:
        pl.semaphore_signal(barrier, inc=1, device_id=dev, device_id_type=MESH)

    count = [0]
    started = []

    def send(src, dst, dev):
        k = count[0]
        count[0] += 1
        copy = pltpu.make_async_remote_copy(
            src_ref=src, dst_ref=dst, send_sem=ssem.at[k], recv_sem=rsem.at[k], device_id=dev, device_id_type=MESH
        )
        copy.start()
        started.append(copy)
        return copy

    def drain(keep=0):
        while len(started) > keep:
            started.pop(0).wait_send()

    def arrived(copies):
        for copy in copies:
            copy.wait_recv()

    fetch[0].wait()
    seen = jnp.int32(0)
    place = [(jnp.int32(0), jnp.int32(0))] * SLOTS
    for p in range(RT * CT):
        there = it[p % CT, p // CT] > 0
        slot = jnp.where(there, seen, SLOTS)
        tabs[core * 16, p] = 2 * slot
        ctabs[me_row, p] = 2 * slot
        for s in range(min(p + 1, SLOTS)):
            i, k = place[s]
            place[s] = (jnp.where(slot == s, p // CT, i), jnp.where(slot == s, p % CT, k))
        seen = seen + there.astype(jnp.int32)
    fetch[1].wait()
    for s in range(SLOTS):
        i, k = place[s]
        tile = jnp.where(k == 0, mk[i, :, :T], mk[i, :, T:]).reshape(2, HALF, T)
        own0[0, core, 2 * s : 2 * s + 2] = tile
        c0[0, 2 * s : 2 * s + 2] = tile
    pl.semaphore_wait(barrier, len(zdevs) + 2 + len(peers))

    front, back, whole = (0, FRONT), (FRONT, PACKED - FRONT), (0, PACKED)
    streams = {"A": (0, back), "B": (0, front), "C": (1, front)}
    ring, crossed, handed = {}, {}, {}

    def at(d, side, o, part):
        return blocks[o][d].at[side % blocks[o][d].shape[0], core, pl.ds(*part)]

    def hop(name, d):
        o, (lo, n) = streams[name]
        h = n // 2
        lower, upper = (lo, h), (lo + h, n - h)
        if d > 1:
            arrived(ring[name, d - 1][0])
        parts = [(lower, upper)] if d == 4 else [(lower, upper), (upper, lower)] if d == 3 else [((lo, n), (lo, n))]
        pairs = [
            [send(at(d - 1, 0, o, a), at(d, 0, o, a), up), send(at(d - 1, 1, o, b), at(d, 1, o, b), down)] for a, b in parts
        ]
        ring[name, d] = (pairs[0], sum(pairs[1:], []))

    def ringed(name, d):
        first, rest = ring[name, d]
        arrived(first + rest if d == 4 else rest)

    def cross(d):
        src, dst = [blocks[o][d].at[:, core, pl.ds(*back)] for o in (0, 1)]
        crossed[d] = send(src, dst, xdev)

    def hand(d, o):
        src = blocks[o][d].at[:, core, pl.ds(*whole)]
        handed[d, o] = send(src, src, cdev)

    def column(ref, n, b):
        def step(i, _):
            for k in range(CT):
                rows = pl.ds(pl.multiple_of(b * BLOCK + i * T, T), T)
                rhs[rows, k * T : (k + 1) * T] = ref[n, pl.ds(ctabs[b, i * CT + k], 2)].reshape(T, T)
            return 0

        lax.fori_loop(0, RT, step, 0)

    def multiply(d, side, o, first=False):
        owner = (z + (NZ - d if side == 0 else d)) % NZ

        def unpack(i, _):
            for c in (0, 1):
                for k in range(CT):
                    slot = tabs[c * 16 + (d + 4 if side else d) * 2 + o, i * CT + k]
                    tile = blocks[o][d][side, c, pl.ds(slot, 2)].reshape(T, T)
                    lhs[pl.ds(pl.multiple_of(i * T, T), T), c * WIDTH + k * T : c * WIDTH + (k + 1) * T] = tile
            return 0

        lax.fori_loop(0, RT, unpack, 0)
        half = (1 - xh) if o else xh
        rows = pl.ds(pl.multiple_of(owner * BLOCK + half * (2 * WIDTH), 2 * WIDTH), 2 * WIDTH)
        part = jnp.dot(lhs[...], rhs[rows, :], preferred_element_type=jnp.float32)
        acc[...] = part if first else acc[...] + part

    tx = send(tabs.at[pl.ds(core * 16, 1)], tabs.at[pl.ds(core * 16 + 1, 1)], xdev)
    hop("A", 1)
    px = send(at(0, 0, 0, front), at(0, 0, 1, front), xdev)
    ct = [send(ctabs.at[pl.ds(me_row, 1)], ctabs.at[pl.ds(me_row, 1)], dev) for dev in peers]
    lower, upper = pl.ds(0, SLOTS), pl.ds(SLOTS, SLOTS)
    y1 = [send(c0.at[0, part], cy.at[n, part], dev) for n, dev, part in [(0, yup, lower), (1, ydown, upper)]]
    hop("B", 1)
    y1 += [send(c0.at[0, part], cy.at[n, part], dev) for n, dev, part in [(0, yup, upper), (1, ydown, lower)]]
    xl = [send(c0.at[0, part], cx.at[0, part], xldev) for part in (lower, upper)]
    hand(0, 0)
    cross(0)

    zero = jnp.zeros((2, HALF, T), jnp.bfloat16)
    for ref in blocks[0] + blocks[1]:
        for n in range(ref.shape[0]):
            for c in (0, 1):
                ref[n, c, PACKED : PACKED + 2] = zero
    for ref in (c0, cx, cy, cyx, c2, c2x):
        for n in range(ref.shape[0]):
            ref[n, PACKED : PACKED + 2] = zero

    tx.wait_recv()
    pair = tabs.at[pl.ds(core * 16, 2)]
    tz = []
    for j, dev in enumerate(zdevs):
        rel = j + 1 if j < 4 else 12 - (j + 1)
        tz.append(send(pair, tabs.at[pl.ds(core * 16 + rel * 2, 2)], dev))
    hop("A", 2)
    cross(1)
    px.wait_recv()
    hop("C", 1)
    arrived(y1[:2])
    y2 = [send(cy.at[0, lower], c2.at[0, lower], yup), send(cy.at[1, upper], c2.at[0, upper], ydown)]
    hop("B", 2)
    xl[0].wait_recv()
    y1x = [send(cx.at[0, lower], cyx.at[n, lower], dev) for n, dev in enumerate((yup, ydown))]
    arrived(ct)
    column(c0, 0, me_row)
    xl[1].wait_recv()
    y1x += [send(cx.at[0, upper], cyx.at[n, upper], dev) for n, dev in enumerate((yup, ydown))]
    hand(1, 0)
    hop("A", 3)
    cross(2)
    below, above, across = (y + NY - 1) % NY, (y + 1) % NY, (y + 2) % NY
    column(cx, 0, (1 - xlo) * NY + y)
    arrived(y1[2:])
    column(cy, 0, xlo * NY + below)
    column(cy, 1, xlo * NY + above)
    hop("C", 2)
    arrived([y1x[0], y1x[3]])
    y2x = [send(cyx.at[0, lower], c2x.at[0, lower], yup), send(cyx.at[1, upper], c2x.at[0, upper], ydown)]
    arrived(tz)
    mine = tabs.at[pl.ds(core * 16, 16)]
    tc = send(mine, mine, cdev)
    crossed[0].wait_recv()
    hand(0, 1)
    arrived(y1x[1:3])
    column(cyx, 0, (1 - xlo) * NY + below)
    column(cyx, 1, (1 - xlo) * NY + above)
    hop("B", 3)
    hand(2, 0)
    arrived(y2)
    column(c2, 0, xlo * NY + across)
    hop("A", 4)
    ringed("A", 3)
    cross(3)
    crossed[1].wait_recv()
    hand(1, 1)
    drain(20)
    arrived(y2x)
    column(c2x, 0, (1 - xlo) * NY + across)
    tc.wait_recv()
    handed[0, 0].wait_recv()
    multiply(0, 0, 0, first=True)
    handed[1, 0].wait_recv()
    multiply(1, 0, 0)
    hop("C", 3)
    multiply(1, 1, 0)
    hop("B", 4)
    ringed("B", 3)
    hand(3, 0)
    crossed[2].wait_recv()
    hand(2, 1)
    handed[2, 0].wait_recv()
    multiply(2, 0, 0)
    multiply(2, 1, 0)
    ringed("A", 4)
    cross(4)
    handed[0, 1].wait_recv()
    multiply(0, 0, 1)
    hop("C", 4)
    handed[1, 1].wait_recv()
    multiply(1, 0, 1)
    multiply(1, 1, 1)
    handed[2, 1].wait_recv()
    ringed("C", 3)
    crossed[3].wait_recv()
    hand(3, 1)
    multiply(2, 0, 1)
    multiply(2, 1, 1)
    ringed("B", 4)
    hand(4, 0)
    handed[3, 0].wait_recv()
    multiply(3, 0, 0)
    multiply(3, 1, 0)
    crossed[4].wait_recv()
    ringed("C", 4)
    hand(4, 1)
    drain(2)
    handed[3, 1].wait_recv()
    multiply(3, 0, 1)
    multiply(3, 1, 1)
    handed[4, 0].wait_recv()
    multiply(4, 0, 0)
    handed[4, 1].wait_recv()
    multiply(4, 0, 1)

    lane = lax.broadcasted_iota(jnp.int32, (1, WIDTH), 1)
    fetch[2].wait()

    def square(i, total):
        rows = pl.ds(pl.multiple_of(i * T, T), T)
        keep = jnp.where(lane < T, kt[0, i], kt[1, i]).astype(jnp.float32)
        v = acc[rows, :]
        v = v * v * keep
        acc[rows, :] = v
        return total + jnp.sum(v.reshape(T // 8, 8, WIDTH), axis=0)

    cs[me_row] = lax.fori_loop(0, RT, square, jnp.zeros((8, WIDTH), jnp.float32))
    sums = [send(cs.at[me_row], cs.at[me_row], dev) for dev in peers]
    drain(len(sums))
    arrived(sums)
    total = jnp.sum(jnp.sum(cs[...], axis=0), axis=0, keepdims=True)
    scale = jnp.float32(NZ * BLOCK) / total

    def finish(i, _):
        rows = pl.ds(pl.multiple_of(i * T, T), T)
        out[rows, :] = (acc[rows, :] * scale).astype(jnp.bfloat16)
        return 0

    lax.fori_loop(0, RT, finish, 0)
    drain()


def body(markov, input_tiles, keep_tiles):
    hbm = pl.BlockSpec(memory_space=pltpu.HBM)

    def packed(*lead):
        return pltpu.VMEM((*lead, PACKED + 2, HALF, T), jnp.bfloat16)

    sides = [packed(1, 2), packed(2, 2), packed(2, 2), packed(2, 2), packed(1, 2)]

    return pl.pallas_call(
        kernel,
        out_shape=jax.ShapeDtypeStruct(markov.shape, jnp.bfloat16),
        in_specs=[hbm, hbm, hbm],
        out_specs=pl.BlockSpec(memory_space=pltpu.VMEM),
        scratch_shapes=sides + sides
        + [packed(1), packed(1), packed(2), packed(2), packed(1), packed(1)]
        + [
            pltpu.VMEM((NZ * BLOCK, WIDTH), jnp.bfloat16),
            pltpu.VMEM((BLOCK, 2 * WIDTH), jnp.bfloat16),
            pltpu.VMEM((BLOCK, WIDTH), jnp.float32),
            pltpu.VMEM((NROW, 8, WIDTH), jnp.float32),
            pltpu.VMEM((RT, T, WIDTH), jnp.bfloat16),
            pltpu.SMEM((CT, RT), jnp.int32),
            pltpu.SMEM((CT, RT), jnp.int32),
            pltpu.SMEM((32, 128), jnp.int32),
            pltpu.SMEM((NROW, 128), jnp.int32),
            pltpu.SemaphoreType.DMA((3,)),
            pltpu.SemaphoreType.DMA((COPIES,)),
            pltpu.SemaphoreType.DMA((COPIES,)),
        ],
        compiler_params=pltpu.CompilerParams(
            collective_id=0, has_side_effects=True, vmem_limit_bytes=40 * 2**20
        ),
        name="cluster_step",
    )(markov.reshape(RT, T, WIDTH), input_tiles.T, keep_tiles.T)


def solution(mesh):
    specs = (P("row", "col"), P("row", "col"), P("row", "col"))
    return jax.shard_map(body, mesh=mesh, in_specs=specs, out_specs=P("row", "col"), check_vma=False)
```

time: 262 us -> 55.2 us (0.21)
  waiting for transfers between devices: 213 us -> 0 us
  Pallas kernels: 0 us -> 51.9 us
  blocking collectives: 14.9 us -> 0 us
  between operations: 13.4 us -> 0.01 us
  matrix products: 9.34 us -> 0 us
  other arithmetic: 4.16 us -> 0 us
    all_gather x2 -> x0, waiting for transfers between devices: 212 us -> none  [the longest x1 155 us: body(): lax.all_gather(masked, 'col', axis=1, tiled=True)]
    pallas_call x0 -> x1, Pallas kernels: none -> 51.9 us  [body(): pl.pallas_call(kernel, out_shape=jax.ShapeDtypeStruct(markov.shape, jnp.b...]
    psum x1 -> x0, blocking collectives: 14.9 us -> none  [body(): colsum = lax.psum(jnp.sum(inflated, axis=0), 'row')]
    dot_general x1 -> x0, matrix products: 9.34 us -> none  [body(): jnp.dot(lax.all_gather(masked, 'col', axis=1, tiled=True), right_whole, p...]
    broadcast_in_dim x4 -> x0, local copies, waits for them, and re-layouts: 4.25 us -> none  [the longest x2 4.17 us: spread(): jnp.repeat(jnp.repeat(pattern, tile_width, axis=0), tile_width, axis=1)]
  transfers between devices with their start and end apart: 2 -> 0, of which waited for: 2 -> 0; matrix products, arithmetic and copies ran while one was open for 0% -> 0% of each run, Pallas kernels for 0% -> 0%
where the time goes in v2:
time: 55.2 us; the launch traced here: 54.5 us
  Pallas kernels  51.9 us (94%)
  local copies, waits for them, and re-layouts  2.53 us (5%)
    pallas_call x1, Pallas kernels, body(): pl.pallas_call(kernel, out_shape=jax.ShapeDtypeStruct(markov.shape, jnp.b...  51.9 us
    unnamed x7, local copies, waits for them, and re-layouts  2.53 us

profile of v2, /device:TPU:1, one launch (start us, length us, event | category | flops | bytes accessed | tf_op | source)
XLA Modules:
  0.0 54.5 jit_solution(13719254873759913143)
XLA Ops:
  0.0 0.0 copy-start.2
  0.0 0.0 copy-start.1
  0.0 0.7 %copy-done.2 = s32[8,2]{0,1:T(2,128)S(1)} copy-done((s32[8,2]{0,1:T(2,128)S(1)}, s32[8,2]{0,1:T(2,128)}, u32[]{:S(2)}) %copy-start.2) | copy-done | bytes 88
  0.7 0.0 copy-done.1
  0.7 0.0 copy-start
  0.7 1.0 %copy-done = bf16[1024,256]{1,0:T(8,128)(2,1)S(1)} copy-done((bf16[1024,256]{1,0:T(8,128)(2,1)S(1)}, bf16[1024,256]{1,0:T(8,128)(2,1)}, u32[]{:S(2)}) %copy-start) | copy-done | bytes 524312
  1.7 51.9 %cluster_step.1 = bf16[1024,256]{1,0:T(8,128)(2,1)S(1)} custom-call(bf16[8,128,256]{2,1,0:T(8,128)(2,1)S(1)} %bitcast.3, s32[2,8]{1,0:T(2,128)S(1)} %bitcast.4, s32[2,8]{1,0:T(2,128)S(1)} %bitcast.5), custom_call_target="tpu_custom_call" | custom-call | tf_op jit(solution)/shard_map/cluster_step/pallas_call | solution.py:295
  53.7 0.8 %copy.5 = bf16[1024,256]{1,0:T(8,128)(2,1)} copy(bf16[1024,256]{1,0:T(8,128)(2,1)S(1)} %cluster_step.1) | data formatting | bytes 1048576
Async XLA Ops:
  0.0 0.7 %copy-start.2 = (s32[8,2]{0,1:T(2,128)S(1)}, s32[8,2]{0,1:T(2,128)}, u32[]{:S(2)}) copy-start(s32[8,2]{0,1:T(2,128)} %param.5) | copy-start | bytes 196
  0.0 0.7 %copy-start.1 = (s32[8,2]{0,1:T(2,128)S(1)}, s32[8,2]{0,1:T(2,128)}, u32[]{:S(2)}) copy-start(s32[8,2]{0,1:T(2,128)} %param.4) | copy-start | bytes 196
  0.7 1.0 %copy-start = (bf16[1024,256]{1,0:T(8,128)(2,1)S(1)}, bf16[1024,256]{1,0:T(8,128)(2,1)}, u32[]{:S(2)}) copy-start(bf16[1024,256]{1,0:T(8,128)(2,1)} %param.3) | copy-start | bytes 1572868

commit v3 on v2

v3 whole, which is shorter than its diff:
```python
import jax
import jax.numpy as jnp
from jax import lax
from jax.experimental import pallas as pl
from jax.experimental.pallas import tpu as pltpu
from jax.sharding import PartitionSpec as P

MESH = pl.DeviceIdType.MESH
T = 128
RT, CT = 8, 2
SLOTS = 8
HALF = T // 2
PACKED = 2 * SLOTS
FRONT = 9
NZ, NY, NROW = 8, 4, 8
BLOCK = RT * T
WIDTH = CT * T
COPIES = 112
EARLY = 6


def kernel(
    mk_hbm, it_hbm, kt_hbm, out, own0, own1, own2, own3, own4, far0, far1, far2, far3, mine4, theirs4, c0, cx, cy, cyx, c2, c2x,
    rhs, lhs, acc, cs, mk, it, kt, tabs, ctabs, insem, ssem, rsem,
):
    blocks = ((own0, own1, own2, own3, own4), (far0, far1, far2, far3, None))
    me_row, me_col = lax.axis_index("row"), lax.axis_index("col")
    xlo, y = me_row // NY, me_row % NY
    z, xh, core = me_col // 4, (me_col // 2) % 2, me_col % 2
    zdevs = [(me_row, ((z + d) % NZ) * 4 + xh * 2 + core) for d in range(1, NZ)]
    up, down = zdevs[0], zdevs[-1]
    at_y = [[(x * NY + (y + d) % NY, me_col) for d in range(NY)] for x in (xlo, 1 - xlo)]
    yup, ydown = at_y[0][1], at_y[0][3]
    xdev = (me_row, z * 4 + (1 - xh) * 2 + core)
    xldev = at_y[1][0]
    cdev = (me_row, z * 4 + xh * 2 + (1 - core))
    peers = at_y[0][1:] + at_y[1]

    inputs = [(it_hbm, it), (mk_hbm, mk), (kt_hbm, kt)]
    fetch = [pltpu.make_async_copy(src, dst, insem.at[n]) for n, (src, dst) in enumerate(inputs)]
    for copy in fetch:
        copy.start()
    barrier = pltpu.get_barrier_semaphore()
    near = [up, down, xdev, cdev, yup, ydown, xldev]
    for dev in near:
        pl.semaphore_signal(barrier, inc=1, device_id=dev, device_id_type=MESH)

    count = [0]
    started = []

    def send(src, dst, dev):
        k = count[0]
        count[0] += 1
        copy = pltpu.make_async_remote_copy(
            src_ref=src, dst_ref=dst, send_sem=ssem.at[k], recv_sem=rsem.at[k], device_id=dev, device_id_type=MESH
        )
        copy.start()
        started.append(copy)
        return copy

    def drain(keep=0):
        while len(started) > keep:
            started.pop(0).wait_send()

    def arrived(copies):
        for copy in copies:
            copy.wait_recv()

    fetch[0].wait()
    seen = jnp.int32(0)
    place = [(jnp.int32(0), jnp.int32(0))] * SLOTS
    for p in range(RT * CT):
        there = it[p % CT, p // CT] > 0
        slot = jnp.where(there, seen, SLOTS)
        tabs[core * 16, p] = 2 * slot
        ctabs[me_row, p] = 2 * slot
        for s in range(min(p + 1, SLOTS)):
            i, k = place[s]
            place[s] = (jnp.where(slot == s, p // CT, i), jnp.where(slot == s, p % CT, k))
        seen = seen + there.astype(jnp.int32)
    fetch[1].wait()
    for s in range(SLOTS):
        i, k = place[s]
        tile = jnp.where(k == 0, mk[i, :, :T], mk[i, :, T:]).reshape(2, HALF, T)
        own0[0, core, 2 * s : 2 * s + 2] = tile
        c0[0, 2 * s : 2 * s + 2] = tile
    pl.semaphore_wait(barrier, len(near))

    front, back, whole = (0, FRONT), (FRONT, PACKED - FRONT), (0, PACKED)
    streams = {"A": (0, back), "B": (0, front), "C": (1, front)}
    ring, crossed, handed = {}, {}, {}

    def at(d, side, o, part):
        if o and d == 4:
            return mine4.at[pl.ds(*part)]
        return blocks[o][d].at[side % blocks[o][d].shape[0], core, pl.ds(*part)]

    def halves_of(name):
        o, (lo, n) = streams[name]
        return (lo, n // 2), (lo + n // 2, n - n // 2)

    def rel(d, side):
        return max(2 * d - 1, 0) + (side if 0 < d < 4 else 0)

    def table_of(o, d, side, n=1, c=core):
        return tabs.at[pl.ds(c * 16 + o * 8 + rel(d, side), n)]

    def both(name, d, a, b):
        o = streams[name][0]
        return [send(at(d - 1, 0, o, a), at(d, 0, o, a), up), send(at(d - 1, 1, o, b), at(d, 1, o, b), down)]

    def hop(name, d):
        if d > 1:
            arrived(ring[name, d - 1])
        if name != "B":
            o = streams[name][0]
            arrived(ring.get((name, "table", d - 1), []))
            ways = [(0, up), (1, down)][: 2 if d < 4 else 1]
            ring[name, "table", d] = [send(table_of(o, d - 1, side), table_of(o, d, side), dev) for side, dev in ways]
        whole = streams[name][1]
        ring[name, d] = both(name, d, *(halves_of(name) if d > 2 else (whole, whole)))

    def rest(name):
        ring[name, "rest"] = both(name, 3, *reversed(halves_of(name)))

    def cross(d):
        if d == 4:
            src, dst = at(4, 0, 0, back), at(4, 0, 1, back)
        else:
            src, dst = [blocks[o][d].at[:, core, pl.ds(*back)] for o in (0, 1)]
        crossed[d] = send(src, dst, xdev)

    def hand(d, o):
        table = table_of(o, d, 0, 2 if 0 < d < 4 else 1)
        src = blocks[o][d].at[:, core, pl.ds(*whole)]
        handed[d, o] = [send(table, table, cdev), send(src, src, cdev)]

    def column(ref, n, b):
        def step(i, _):
            for k in range(CT):
                rows = pl.ds(pl.multiple_of(b * BLOCK + i * T, T), T)
                rhs[rows, k * T : (k + 1) * T] = ref[n, pl.ds(ctabs[b, i * CT + k], 2)].reshape(T, T)
            return 0

        lax.fori_loop(0, RT, step, 0)

    place_of = {}

    def unpack(d, side, o, turn=None):
        place_of[d, side, o] = n = len(place_of) if turn is None else EARLY + turn

        def step(i, _):
            for c in (0, 1):
                for k in range(CT):
                    slot = tabs[c * 16 + o * 8 + rel(d, side), i * CT + k]
                    tile = blocks[o][d][side, c, pl.ds(slot, 2)].reshape(T, T)
                    lhs[n, pl.ds(pl.multiple_of(i * T, T), T), c * WIDTH + k * T : c * WIDTH + (k + 1) * T] = tile
            return 0

        lax.fori_loop(0, RT, step, 0)

    def multiply(d, side, o, first=False):
        owner = (z + (NZ - d if side == 0 else d)) % NZ
        half = (1 - xh) if o else xh
        rows = pl.ds(pl.multiple_of(owner * BLOCK + half * (2 * WIDTH), 2 * WIDTH), 2 * WIDTH)
        part = jnp.dot(lhs[place_of[d, side, o]], rhs[rows, :], preferred_element_type=jnp.float32)
        acc[...] = part if first else acc[...] + part

    def late(d, side, o):
        unpack(d, side, o, side)
        multiply(d, side, o)

    def multiply_last(ref, c):
        def step(i, _):
            for k in range(CT):
                tile = ref[pl.ds(tabs[c * 16 + 8 + rel(4, 0), i * CT + k], 2)].reshape(T, T)
                lhs[EARLY, pl.ds(pl.multiple_of(i * T, T), T), k * T : (k + 1) * T] = tile
            return 0

        lax.fori_loop(0, RT, step, 0)
        base = ((z + 4) % NZ) * BLOCK + (1 - xh) * (2 * WIDTH) + c * WIDTH
        rows = pl.ds(pl.multiple_of(base, WIDTH), WIDTH)
        acc[...] += jnp.dot(lhs[EARLY, :, :WIDTH], rhs[rows, :], preferred_element_type=jnp.float32)

    def ctable(b, devs):
        return [send(ctabs.at[pl.ds(b, 1)], ctabs.at[pl.ds(b, 1)], dev) for dev in devs]

    hop("A", 1)
    tx = send(table_of(0, 0, 0), table_of(1, 0, 0), xdev)
    px = send(at(0, 0, 0, front), at(0, 0, 1, front), xdev)
    lower, upper = pl.ds(0, SLOTS), pl.ds(SLOTS, SLOTS)
    ct = ctable(me_row, [yup, ydown])
    y1 = [send(c0.at[0, part], cy.at[n, part], dev) for n, dev, part in [(0, yup, lower), (1, ydown, upper)]]
    hop("B", 1)
    y1 += [send(c0.at[0, part], cy.at[n, part], dev) for n, dev, part in [(0, yup, upper), (1, ydown, lower)]]
    ctx = ctable(me_row, [xldev])
    xl = [send(c0.at[0, part], cx.at[0, part], xldev) for part in (lower, upper)]
    hand(0, 0)
    cross(0)

    zero = jnp.zeros((2, HALF, T), jnp.bfloat16)
    for ref in blocks[0] + blocks[1][:4]:
        for n in range(ref.shape[0]):
            for c in (0, 1):
                ref[n, c, PACKED : PACKED + 2] = zero
    for ref in (mine4, theirs4):
        ref[PACKED : PACKED + 2] = zero
    for ref in (c0, cx, cy, cyx, c2, c2x):
        for n in range(ref.shape[0]):
            ref[n, PACKED : PACKED + 2] = zero

    below, above, across = (y + NY - 1) % NY, (y + 1) % NY, (y + 2) % NY
    other = (1 - xlo) * NY
    hop("A", 2)
    cross(1)
    arrived([tx, px])
    hop("C", 1)
    arrived(y1[:2] + ct)
    ct2 = ctable(xlo * NY + below, [yup])
    y2 = [send(cy.at[0, lower], c2.at[0, lower], yup), send(cy.at[1, upper], c2.at[0, upper], ydown)]
    hop("B", 2)
    hand(1, 0)
    arrived(ctx + xl[:1])
    ctyx = ctable(other + y, [yup, ydown])
    y1x = [send(cx.at[0, lower], cyx.at[n, lower], dev) for n, dev in enumerate((yup, ydown))]
    column(c0, 0, me_row)
    hop("A", 3)
    rest("A")
    cross(2)
    arrived(xl[1:])
    y1x += [send(cx.at[0, upper], cyx.at[n, upper], dev) for n, dev in enumerate((yup, ydown))]
    column(cx, 0, other + y)
    arrived(y1[2:])
    column(cy, 0, xlo * NY + below)
    column(cy, 1, xlo * NY + above)
    arrived(handed[0, 0])
    unpack(0, 0, 0)
    hop("C", 2)
    crossed[0].wait_recv()
    hand(0, 1)
    arrived(handed[1, 0])
    unpack(1, 0, 0)
    unpack(1, 1, 0)
    arrived([y1x[0], y1x[3]] + ctyx)
    ct2x = ctable(other + below, [yup])
    y2x = [send(cyx.at[0, lower], c2x.at[0, lower], yup), send(cyx.at[1, upper], c2x.at[0, upper], ydown)]
    hop("B", 3)
    hand(2, 0)
    arrived(y1x[1:3])
    column(cyx, 0, other + below)
    column(cyx, 1, other + above)
    hop("A", 4)
    arrived(ring["A", "rest"])
    cross(3)
    arrived(handed[0, 1])
    unpack(0, 0, 1)
    arrived(y2 + ct2)
    column(c2, 0, xlo * NY + across)
    crossed[1].wait_recv()
    hand(1, 1)
    arrived(handed[2, 0])
    unpack(2, 0, 0)
    unpack(2, 1, 0)
    drain(24)
    arrived(y2x + ct2x)
    column(c2x, 0, other + across)
    multiply(0, 0, 0, first=True)
    hop("C", 3)
    rest("B")
    rest("C")
    multiply(1, 0, 0)
    multiply(1, 1, 0)
    multiply(0, 0, 1)
    hop("B", 4)
    drain(20)
    crossed[2].wait_recv()
    hand(2, 1)
    multiply(2, 0, 0)
    multiply(2, 1, 0)
    arrived(ring["A", 4])
    cross(4)
    arrived(handed[1, 1])
    late(1, 0, 1)
    late(1, 1, 1)
    hop("C", 4)
    drain(16)
    arrived(ring["B", "rest"])
    hand(3, 0)
    arrived(handed[2, 1])
    late(2, 0, 1)
    late(2, 1, 1)
    arrived(ring["C", "rest"])
    crossed[3].wait_recv()
    hand(3, 1)
    arrived(handed[3, 0])
    late(3, 0, 0)
    late(3, 1, 0)
    arrived(ring["B", 4] + ring["A", "table", 4])
    hand(4, 0)
    drain(12)
    arrived(handed[3, 1])
    late(3, 0, 1)

    def hand_last(lo, n):
        return send(mine4.at[pl.ds(lo, n)], theirs4.at[pl.ds(lo, n)], cdev)

    crossed[4].wait_recv()
    last = [hand_last(*back)]
    late(3, 1, 1)
    for copy, part in zip(ring["C", 4], halves_of("C")):
        copy.wait_recv()
        last.append(hand_last(*part))
    arrived(ring["C", "table", 4])
    last.append(send(table_of(1, 4, 0), table_of(1, 4, 0), cdev))
    arrived(handed[4, 0])
    late(4, 0, 0)
    multiply_last(mine4, core)
    drain(4)
    arrived(last)
    multiply_last(theirs4, 1 - core)

    lane = lax.broadcasted_iota(jnp.int32, (1, WIDTH), 1)
    fetch[2].wait()

    def square(i, total):
        rows = pl.ds(pl.multiple_of(i * T, T), T)
        keep = jnp.where(lane < T, kt[0, i], kt[1, i]).astype(jnp.float32)
        v = acc[rows, :]
        v = v * v * keep
        acc[rows, :] = v
        return total + jnp.sum(v.reshape(T // 8, 8, WIDTH), axis=0)

    part = lax.fori_loop(0, RT, square, jnp.zeros((8, WIDTH), jnp.float32))
    cs[me_row] = jnp.sum(part, axis=0, keepdims=True)
    sums = [send(cs.at[me_row], cs.at[me_row], dev) for dev in peers]
    drain(len(sums))
    arrived(sums)
    total = jnp.sum(cs[...], axis=0)
    scale = jnp.float32(NZ * BLOCK) / total

    def finish(i, _):
        rows = pl.ds(pl.multiple_of(i * T, T), T)
        out[rows, :] = (acc[rows, :] * scale).astype(jnp.bfloat16)
        return 0

    lax.fori_loop(0, RT, finish, 0)
    drain()


def body(markov, input_tiles, keep_tiles):
    hbm = pl.BlockSpec(memory_space=pltpu.HBM)

    def packed(*lead):
        return pltpu.VMEM((*lead, PACKED + 2, HALF, T), jnp.bfloat16)

    sides = [packed(1, 2), packed(2, 2), packed(2, 2), packed(2, 2), packed(1, 2)]

    return pl.pallas_call(
        kernel,
        out_shape=jax.ShapeDtypeStruct(markov.shape, jnp.bfloat16),
        in_specs=[hbm, hbm, hbm],
        out_specs=pl.BlockSpec(memory_space=pltpu.VMEM),
        scratch_shapes=sides + sides[:4]
        + [packed(), packed()]
        + [packed(1), packed(1), packed(2), packed(2), packed(1), packed(1)]
        + [
            pltpu.VMEM((NZ * BLOCK, WIDTH), jnp.bfloat16),
            pltpu.VMEM((EARLY + 2, BLOCK, 2 * WIDTH), jnp.bfloat16),
            pltpu.VMEM((BLOCK, WIDTH), jnp.float32),
            pltpu.VMEM((NROW, 1, WIDTH), jnp.float32),
            pltpu.VMEM((RT, T, WIDTH), jnp.bfloat16),
            pltpu.SMEM((CT, RT), jnp.int32),
            pltpu.SMEM((CT, RT), jnp.int32),
            pltpu.SMEM((32, 128), jnp.int32),
            pltpu.SMEM((NROW, 128), jnp.int32),
            pltpu.SemaphoreType.DMA((3,)),
            pltpu.SemaphoreType.DMA((COPIES,)),
            pltpu.SemaphoreType.DMA((COPIES,)),
        ],
        compiler_params=pltpu.CompilerParams(
            collective_id=0, has_side_effects=True, vmem_limit_bytes=53 * 2**20
        ),
        name="cluster_step",
    )(markov.reshape(RT, T, WIDTH), input_tiles.T, keep_tiles.T)


def solution(mesh):
    specs = (P("row", "col"), P("row", "col"), P("row", "col"))
    return jax.shard_map(body, mesh=mesh, in_specs=specs, out_specs=P("row", "col"), check_vma=False)
```

time: 55.2 us -> 53.1 us (0.962); the launches traced: 54.5 us -> 53 us
  local copies, waits for them, and re-layouts: 2.53 us -> 1.49 us
    unnamed x7 -> x5, local copies, waits for them, and re-layouts: 2.53 us -> 1.49 us
where the time goes in v3:
time: 53.1 us; the launch traced here: 53 us
  Pallas kernels  51.5 us (97%)
  local copies, waits for them, and re-layouts  1.49 us (3%)
    pallas_call x1, Pallas kernels, body(): pl.pallas_call(kernel, out_shape=jax.ShapeDtypeStruct(markov.shape, jnp.b...  51.5 us
    unnamed x5, local copies, waits for them, and re-layouts  1.49 us

profile of v3, /device:TPU:1, one launch (start us, length us, event | category | flops | bytes accessed | tf_op | source)
XLA Modules:
  0.0 53.0 jit_solution(15465895155475630047)
XLA Ops:
  0.0 0.0 copy-start.1
  0.0 0.0 copy-start
  0.0 0.7 %copy-done.1 = s32[8,2]{0,1:T(2,128)S(1)} copy-done((s32[8,2]{0,1:T(2,128)S(1)}, s32[8,2]{0,1:T(2,128)}, u32[]{:S(2)}) %copy-start.1) | copy-done | bytes 88
  0.7 0.0 copy-done
  0.7 51.5 %cluster_step.1 = bf16[1024,256]{1,0:T(8,128)(2,1)S(1)} custom-call(bf16[8,128,256]{2,1,0:T(8,128)(2,1)} %bitcast.5, s32[2,8]{1,0:T(2,128)S(1)} %bitcast.3, s32[2,8]{1,0:T(2,128)S(1)} %bitcast.4), custom_call_target="tpu_custom_call" | custom-call | tf_op jit(solution)/shard_map/cluster_step/pallas_call | solution.py:358
  52.2 0.8 %copy.5 = bf16[1024,256]{1,0:T(8,128)(2,1)} copy(bf16[1024,256]{1,0:T(8,128)(2,1)S(1)} %cluster_step.1) | data formatting | bytes 1048576
Async XLA Ops:
  0.0 0.7 %copy-start.1 = (s32[8,2]{0,1:T(2,128)S(1)}, s32[8,2]{0,1:T(2,128)}, u32[]{:S(2)}) copy-start(s32[8,2]{0,1:T(2,128)} %param.5) | copy-start | bytes 196
  0.0 0.7 %copy-start = (s32[8,2]{0,1:T(2,128)S(1)}, s32[8,2]{0,1:T(2,128)}, u32[]{:S(2)}) copy-start(s32[8,2]{0,1:T(2,128)} %param.4) | copy-start | bytes 196

commit v4 on v3

--- a/solution.py
+++ b/solution.py
@@ -34,16 +34,17 @@
     xdev = (me_row, z * 4 + (1 - xh) * 2 + core)
     xldev = at_y[1][0]
     cdev = (me_row, z * 4 + xh * 2 + (1 - core))
-    peers = at_y[0][1:] + at_y[1]
-
-    inputs = [(it_hbm, it), (mk_hbm, mk), (kt_hbm, kt)]
-    fetch = [pltpu.make_async_copy(src, dst, insem.at[n]) for n, (src, dst) in enumerate(inputs)]
-    for copy in fetch:
-        copy.start()
+    peers = [at_y[x][d] for x, d in ((1, 2), (1, 1), (1, 3), (0, 2), (1, 0), (0, 1), (0, 3))]
+
     barrier = pltpu.get_barrier_semaphore()
     near = [up, down, xdev, cdev, yup, ydown, xldev]
     for dev in near:
         pl.semaphore_signal(barrier, inc=1, device_id=dev, device_id_type=MESH)
+    inputs = [(it_hbm, it), (kt_hbm, kt)]
+    inputs += [(mk_hbm.at[:, :, pl.ds(k * T, T)], mk.at[pl.ds(k * RT, RT)]) for k in range(CT)]
+    fetch = [pltpu.make_async_copy(src, dst, insem.at[n]) for n, (src, dst) in enumerate(inputs)]
+    for n in (0, 2, 3, 1):
+        fetch[n].start()
 
     count = [0]
     started = []
@@ -68,20 +69,20 @@
 
     fetch[0].wait()
     seen = jnp.int32(0)
-    place = [(jnp.int32(0), jnp.int32(0))] * SLOTS
+    place = [jnp.int32(0)] * SLOTS
     for p in range(RT * CT):
-        there = it[p % CT, p // CT] > 0
+        i, k = p // CT, p % CT
+        there = it[k, i] > 0
         slot = jnp.where(there, seen, SLOTS)
         tabs[core * 16, p] = 2 * slot
         ctabs[me_row, p] = 2 * slot
         for s in range(min(p + 1, SLOTS)):
-            i, k = place[s]
-            place[s] = (jnp.where(slot == s, p // CT, i), jnp.where(slot == s, p % CT, k))
+            place[s] = jnp.where(slot == s, k * RT + i, place[s])
         seen = seen + there.astype(jnp.int32)
-    fetch[1].wait()
+    fetch[2].wait()
+    fetch[3].wait()
     for s in range(SLOTS):
-        i, k = place[s]
-        tile = jnp.where(k == 0, mk[i, :, :T], mk[i, :, T:]).reshape(2, HALF, T)
+        tile = mk[place[s]].reshape(2, HALF, T)
         own0[0, core, 2 * s : 2 * s + 2] = tile
         c0[0, 2 * s : 2 * s + 2] = tile
     pl.semaphore_wait(barrier, len(near))
@@ -146,7 +147,7 @@
 
     place_of = {}
 
-    def unpack(d, side, o, turn=None):
+    def unpack(d, side, o, turn=None, unroll=False):
         place_of[d, side, o] = n = len(place_of) if turn is None else EARLY + turn
 
         def step(i, _):
@@ -157,7 +158,7 @@
                     lhs[n, pl.ds(pl.multiple_of(i * T, T), T), c * WIDTH + k * T : c * WIDTH + (k + 1) * T] = tile
             return 0
 
-        lax.fori_loop(0, RT, step, 0)
+        lax.fori_loop(0, RT, step, 0, unroll=unroll)
 
     def multiply(d, side, o, first=False):
         owner = (z + (NZ - d if side == 0 else d)) % NZ
@@ -265,62 +266,66 @@
     arrived(y2x + ct2x)
     column(c2x, 0, other + across)
     multiply(0, 0, 0, first=True)
+    multiply(1, 0, 0)
     hop("C", 3)
     rest("B")
     rest("C")
-    multiply(1, 0, 0)
     multiply(1, 1, 0)
     multiply(0, 0, 1)
     hop("B", 4)
+    multiply(2, 0, 0)
     drain(20)
     crossed[2].wait_recv()
     hand(2, 1)
-    multiply(2, 0, 0)
     multiply(2, 1, 0)
+    arrived(handed[1, 1])
+    late(1, 0, 1)
     arrived(ring["A", 4])
     cross(4)
-    arrived(handed[1, 1])
-    late(1, 0, 1)
     late(1, 1, 1)
     hop("C", 4)
-    drain(16)
+    arrived(handed[2, 1])
+    late(2, 0, 1)
     arrived(ring["B", "rest"])
     hand(3, 0)
-    arrived(handed[2, 1])
-    late(2, 0, 1)
     late(2, 1, 1)
+    drain(16)
     arrived(ring["C", "rest"])
     crossed[3].wait_recv()
     hand(3, 1)
     arrived(handed[3, 0])
-    late(3, 0, 0)
-    late(3, 1, 0)
+    unpack(3, 0, 0, 0)
+    unpack(3, 1, 0, 1, unroll=True)
+    multiply(3, 0, 0)
+    multiply(3, 1, 0)
     arrived(ring["B", 4] + ring["A", "table", 4])
     hand(4, 0)
     drain(12)
     arrived(handed[3, 1])
     late(3, 0, 1)
+    unpack(3, 1, 1, 1)
 
     def hand_last(lo, n):
         return send(mine4.at[pl.ds(lo, n)], theirs4.at[pl.ds(lo, n)], cdev)
 
     crossed[4].wait_recv()
     last = [hand_last(*back)]
-    late(3, 1, 1)
+    arrived(ring["C", "table", 4])
+    last.append(send(table_of(1, 4, 0), table_of(1, 4, 0), cdev))
     for copy, part in zip(ring["C", 4], halves_of("C")):
         copy.wait_recv()
         last.append(hand_last(*part))
-    arrived(ring["C", "table", 4])
-    last.append(send(table_of(1, 4, 0), table_of(1, 4, 0), cdev))
     arrived(handed[4, 0])
-    late(4, 0, 0)
+    unpack(4, 0, 0, 0, unroll=True)
+    multiply(3, 1, 1)
+    multiply(4, 0, 0)
     multiply_last(mine4, core)
     drain(4)
     arrived(last)
     multiply_last(theirs4, 1 - core)
 
     lane = lax.broadcasted_iota(jnp.int32, (1, WIDTH), 1)
-    fetch[2].wait()
+    fetch[1].wait()
 
     def square(i, total):
         rows = pl.ds(pl.multiple_of(i * T, T), T)
@@ -368,12 +373,12 @@
             pltpu.VMEM((EARLY + 2, BLOCK, 2 * WIDTH), jnp.bfloat16),
             pltpu.VMEM((BLOCK, WIDTH), jnp.float32),
             pltpu.VMEM((NROW, 1, WIDTH), jnp.float32),
-            pltpu.VMEM((RT, T, WIDTH), jnp.bfloat16),
+            pltpu.VMEM((CT * RT, T, T), jnp.bfloat16),
             pltpu.SMEM((CT, RT), jnp.int32),
             pltpu.SMEM((CT, RT), jnp.int32),
             pltpu.SMEM((32, 128), jnp.int32),
             pltpu.SMEM((NROW, 128), jnp.int32),
-            pltpu.SemaphoreType.DMA((3,)),
+            pltpu.SemaphoreType.DMA((4,)),
             pltpu.SemaphoreType.DMA((COPIES,)),
             pltpu.SemaphoreType.DMA((COPIES,)),
         ],

time: 53.1 us -> 52.5 us (0.989)
  Pallas kernels: 51.5 us -> 50.9 us
    pallas_call x1, Pallas kernels: 51.5 us -> 50.9 us  [body(): pl.pallas_call(kernel, out_shape=jax.ShapeDtypeStruct(markov.shape, jnp.b...]
where the time goes in v4:
time: 52.5 us; the launch traced here: 52.4 us
  Pallas kernels  50.9 us (97%)
  local copies, waits for them, and re-layouts  1.49 us (3%)
    pallas_call x1, Pallas kernels, body(): pl.pallas_call(kernel, out_shape=jax.ShapeDtypeStruct(markov.shape, jnp.b...  50.9 us
    unnamed x5, local copies, waits for them, and re-layouts  1.49 us

profile of v4, /device:TPU:1, one launch (start us, length us, event | category | flops | bytes accessed | tf_op | source)
XLA Modules:
  0.0 52.4 jit_solution(12351380569290098985)
XLA Ops:
  0.0 0.0 copy-start.1
  0.0 0.0 copy-start
  0.0 0.7 %copy-done.1 = s32[8,2]{0,1:T(2,128)S(1)} copy-done((s32[8,2]{0,1:T(2,128)S(1)}, s32[8,2]{0,1:T(2,128)}, u32[]{:S(2)}) %copy-start.1) | copy-done | bytes 88
  0.7 0.0 copy-done
  0.7 50.9 %cluster_step.1 = bf16[1024,256]{1,0:T(8,128)(2,1)S(1)} custom-call(bf16[8,128,256]{2,1,0:T(8,128)(2,1)} %bitcast.5, s32[2,8]{1,0:T(2,128)S(1)} %bitcast.3, s32[2,8]{1,0:T(2,128)S(1)} %bitcast.4), custom_call_target="tpu_custom_call" | custom-call | tf_op jit(solution)/shard_map/cluster_step/pallas_call | solution.py:363
  51.6 0.8 %copy.5 = bf16[1024,256]{1,0:T(8,128)(2,1)} copy(bf16[1024,256]{1,0:T(8,128)(2,1)S(1)} %cluster_step.1) | data formatting | bytes 1048576
Async XLA Ops:
  0.0 0.7 %copy-start.1 = (s32[8,2]{0,1:T(2,128)S(1)}, s32[8,2]{0,1:T(2,128)}, u32[]{:S(2)}) copy-start(s32[8,2]{0,1:T(2,128)} %param.5) | copy-start | bytes 196
  0.0 0.7 %copy-start = (s32[8,2]{0,1:T(2,128)S(1)}, s32[8,2]{0,1:T(2,128)}, u32[]{:S(2)}) copy-start(s32[8,2]{0,1:T(2,128)} %param.4) | copy-start | bytes 196

commit v5 on v4

--- a/solution.py
+++ b/solution.py
@@ -171,17 +171,19 @@
         unpack(d, side, o, side)
         multiply(d, side, o)
 
-    def multiply_last(ref, c):
+    def unpack_last(ref, c, n, unroll=False):
         def step(i, _):
             for k in range(CT):
                 tile = ref[pl.ds(tabs[c * 16 + 8 + rel(4, 0), i * CT + k], 2)].reshape(T, T)
-                lhs[EARLY, pl.ds(pl.multiple_of(i * T, T), T), k * T : (k + 1) * T] = tile
+                lhs[n, pl.ds(pl.multiple_of(i * T, T), T), k * T : (k + 1) * T] = tile
             return 0
 
-        lax.fori_loop(0, RT, step, 0)
+        lax.fori_loop(0, RT, step, 0, unroll=unroll)
+
+    def multiply_last(c, n):
         base = ((z + 4) % NZ) * BLOCK + (1 - xh) * (2 * WIDTH) + c * WIDTH
         rows = pl.ds(pl.multiple_of(base, WIDTH), WIDTH)
-        acc[...] += jnp.dot(lhs[EARLY, :, :WIDTH], rhs[rows, :], preferred_element_type=jnp.float32)
+        acc[...] += jnp.dot(lhs[n, :, :WIDTH], rhs[rows, :], preferred_element_type=jnp.float32)
 
     def ctable(b, devs):
         return [send(ctabs.at[pl.ds(b, 1)], ctabs.at[pl.ds(b, 1)], dev) for dev in devs]
@@ -318,11 +320,13 @@
     arrived(handed[4, 0])
     unpack(4, 0, 0, 0, unroll=True)
     multiply(3, 1, 1)
+    unpack_last(mine4, core, 0, unroll=True)
     multiply(4, 0, 0)
-    multiply_last(mine4, core)
+    multiply_last(core, 0)
     drain(4)
     arrived(last)
-    multiply_last(theirs4, 1 - core)
+    unpack_last(theirs4, 1 - core, 1, unroll=True)
+    multiply_last(1 - core, 1)
 
     lane = lax.broadcasted_iota(jnp.int32, (1, WIDTH), 1)
     fetch[1].wait()
@@ -335,7 +339,7 @@
         acc[rows, :] = v
         return total + jnp.sum(v.reshape(T // 8, 8, WIDTH), axis=0)
 
-    part = lax.fori_loop(0, RT, square, jnp.zeros((8, WIDTH), jnp.float32))
+    part = lax.fori_loop(0, RT, square, jnp.zeros((8, WIDTH), jnp.float32), unroll=True)
     cs[me_row] = jnp.sum(part, axis=0, keepdims=True)
     sums = [send(cs.at[me_row], cs.at[me_row], dev) for dev in peers]
     drain(len(sums))
@@ -348,7 +352,7 @@
         out[rows, :] = (acc[rows, :] * scale).astype(jnp.bfloat16)
         return 0
 
-    lax.fori_loop(0, RT, finish, 0)
+    lax.fori_loop(0, RT, finish, 0, unroll=True)
     drain()
 
 

time: 52.5 us -> 52 us (level)
  no operation moved by 1% of the time
where the time goes in v5:
time: 52 us; the launch traced here: 51.9 us
  Pallas kernels  50.4 us (97%)
  local copies, waits for them, and re-layouts  1.49 us (3%)
    pallas_call x1, Pallas kernels, body(): pl.pallas_call(kernel, out_shape=jax.ShapeDtypeStruct(markov.shape, jnp.b...  50.4 us
    unnamed x5, local copies, waits for them, and re-layouts  1.49 us

profile of v5, /device:TPU:1, one launch (start us, length us, event | category | flops | bytes accessed | tf_op | source)
XLA Modules:
  0.0 51.9 jit_solution(18145983453848294191)
XLA Ops:
  0.0 0.0 copy-start.1
  0.0 0.0 copy-start
  0.0 0.7 %copy-done.1 = s32[8,2]{0,1:T(2,128)S(1)} copy-done((s32[8,2]{0,1:T(2,128)S(1)}, s32[8,2]{0,1:T(2,128)}, u32[]{:S(2)}) %copy-start.1) | copy-done | bytes 88
  0.7 0.0 copy-done
  0.7 50.4 %cluster_step.1 = bf16[1024,256]{1,0:T(8,128)(2,1)S(1)} custom-call(bf16[8,128,256]{2,1,0:T(8,128)(2,1)} %bitcast.5, s32[2,8]{1,0:T(2,128)S(1)} %bitcast.3, s32[2,8]{1,0:T(2,128)S(1)} %bitcast.4), custom_call_target="tpu_custom_call" | custom-call | tf_op jit(solution)/shard_map/cluster_step/pallas_call | solution.py:367
  51.1 0.8 %copy.5 = bf16[1024,256]{1,0:T(8,128)(2,1)} copy(bf16[1024,256]{1,0:T(8,128)(2,1)S(1)} %cluster_step.1) | data formatting | bytes 1048576
Async XLA Ops:
  0.0 0.7 %copy-start.1 = (s32[8,2]{0,1:T(2,128)S(1)}, s32[8,2]{0,1:T(2,128)}, u32[]{:S(2)}) copy-start(s32[8,2]{0,1:T(2,128)} %param.5) | copy-start | bytes 196
  0.0 0.7 %copy-start = (s32[8,2]{0,1:T(2,128)S(1)}, s32[8,2]{0,1:T(2,128)}, u32[]{:S(2)}) copy-start(s32[8,2]{0,1:T(2,128)} %param.4) | copy-start | bytes 196

commit v6 on v5

--- a/solution.py
+++ b/solution.py
@@ -132,9 +132,10 @@
         crossed[d] = send(src, dst, xdev)
 
     def hand(d, o):
-        table = table_of(o, d, 0, 2 if 0 < d < 4 else 1)
+        table = table_of(o, 0, 0, 5) if (d, o) == (2, 0) else table_of(o, d, 0, 2 if 0 < d < 4 else 1)
         src = blocks[o][d].at[:, core, pl.ds(*whole)]
-        handed[d, o] = [send(table, table, cdev), send(src, src, cdev)]
+        handed[d, o] = [] if o == 0 and d < 2 else [send(table, table, cdev)]
+        handed[d, o].append(send(src, src, cdev))
 
     def column(ref, n, b):
         def step(i, _):
@@ -193,9 +194,8 @@
     px = send(at(0, 0, 0, front), at(0, 0, 1, front), xdev)
     lower, upper = pl.ds(0, SLOTS), pl.ds(SLOTS, SLOTS)
     ct = ctable(me_row, [yup, ydown])
-    y1 = [send(c0.at[0, part], cy.at[n, part], dev) for n, dev, part in [(0, yup, lower), (1, ydown, upper)]]
+    y1 = [send(c0.at[0, pl.ds(*whole)], cy.at[n, pl.ds(*whole)], dev) for n, dev in enumerate((yup, ydown))]
     hop("B", 1)
-    y1 += [send(c0.at[0, part], cy.at[n, part], dev) for n, dev, part in [(0, yup, upper), (1, ydown, lower)]]
     ctx = ctable(me_row, [xldev])
     xl = [send(c0.at[0, part], cx.at[0, part], xldev) for part in (lower, upper)]
     hand(0, 0)
@@ -218,7 +218,7 @@
     cross(1)
     arrived([tx, px])
     hop("C", 1)
-    arrived(y1[:2] + ct)
+    arrived(y1 + ct)
     ct2 = ctable(xlo * NY + below, [yup])
     y2 = [send(cy.at[0, lower], c2.at[0, lower], yup), send(cy.at[1, upper], c2.at[0, upper], ydown)]
     hop("B", 2)
@@ -233,17 +233,11 @@
     arrived(xl[1:])
     y1x += [send(cx.at[0, upper], cyx.at[n, upper], dev) for n, dev in enumerate((yup, ydown))]
     column(cx, 0, other + y)
-    arrived(y1[2:])
     column(cy, 0, xlo * NY + below)
     column(cy, 1, xlo * NY + above)
-    arrived(handed[0, 0])
-    unpack(0, 0, 0)
     hop("C", 2)
     crossed[0].wait_recv()
     hand(0, 1)
-    arrived(handed[1, 0])
-    unpack(1, 0, 0)
-    unpack(1, 1, 0)
     arrived([y1x[0], y1x[3]] + ctyx)
     ct2x = ctable(other + below, [yup])
     y2x = [send(cyx.at[0, lower], c2x.at[0, lower], yup), send(cyx.at[1, upper], c2x.at[0, upper], ydown)]
@@ -261,7 +255,10 @@
     column(c2, 0, xlo * NY + across)
     crossed[1].wait_recv()
     hand(1, 1)
-    arrived(handed[2, 0])
+    arrived(handed[0, 0] + handed[1, 0] + handed[2, 0])
+    unpack(0, 0, 0)
+    unpack(1, 0, 0)
+    unpack(1, 1, 0)
     unpack(2, 0, 0)
     unpack(2, 1, 0)
     drain(24)

time: 52 us -> 52.7 us (1.013)
  Pallas kernels: 50.4 us -> 51.1 us
    pallas_call x1, Pallas kernels: 50.4 us -> 51.1 us  [body(): pl.pallas_call(kernel, out_shape=jax.ShapeDtypeStruct(markov.shape, jnp.b...]
where the time goes in v6:
time: 52.7 us; the launch traced here: 52.6 us
  Pallas kernels  51.1 us (97%)
  local copies, waits for them, and re-layouts  1.49 us (3%)
    pallas_call x1, Pallas kernels, body(): pl.pallas_call(kernel, out_shape=jax.ShapeDtypeStruct(markov.shape, jnp.b...  51.1 us
    unnamed x5, local copies, waits for them, and re-layouts  1.49 us

profile of v6, /device:TPU:1, one launch (start us, length us, event | category | flops | bytes accessed | tf_op | source)
XLA Modules:
  0.0 52.6 jit_solution(8940706624323603795)
XLA Ops:
  0.0 0.0 copy-start.1
  0.0 0.0 copy-start
  0.0 0.7 %copy-done.1 = s32[8,2]{0,1:T(2,128)S(1)} copy-done((s32[8,2]{0,1:T(2,128)S(1)}, s32[8,2]{0,1:T(2,128)}, u32[]{:S(2)}) %copy-start.1) | copy-done | bytes 88
  0.7 0.0 copy-done
  0.7 51.1 %cluster_step.1 = bf16[1024,256]{1,0:T(8,128)(2,1)S(1)} custom-call(bf16[8,128,256]{2,1,0:T(8,128)(2,1)} %bitcast.5, s32[2,8]{1,0:T(2,128)S(1)} %bitcast.3, s32[2,8]{1,0:T(2,128)S(1)} %bitcast.4), custom_call_target="tpu_custom_call" | custom-call | tf_op jit(solution)/shard_map/cluster_step/pallas_call | solution.py:364
  51.8 0.8 %copy.5 = bf16[1024,256]{1,0:T(8,128)(2,1)} copy(bf16[1024,256]{1,0:T(8,128)(2,1)S(1)} %cluster_step.1) | data formatting | bytes 1048576
Async XLA Ops:
  0.0 0.7 %copy-start.1 = (s32[8,2]{0,1:T(2,128)S(1)}, s32[8,2]{0,1:T(2,128)}, u32[]{:S(2)}) copy-start(s32[8,2]{0,1:T(2,128)} %param.5) | copy-start | bytes 196
  0.0 0.7 %copy-start = (s32[8,2]{0,1:T(2,128)S(1)}, s32[8,2]{0,1:T(2,128)}, u32[]{:S(2)}) copy-start(s32[8,2]{0,1:T(2,128)} %param.4) | copy-start | bytes 196

commit v7 on v5

--- a/solution.py
+++ b/solution.py
@@ -183,7 +183,7 @@
     def multiply_last(c, n):
         base = ((z + 4) % NZ) * BLOCK + (1 - xh) * (2 * WIDTH) + c * WIDTH
         rows = pl.ds(pl.multiple_of(base, WIDTH), WIDTH)
-        acc[...] += jnp.dot(lhs[n, :, :WIDTH], rhs[rows, :], preferred_element_type=jnp.float32)
+        return acc[...] + jnp.dot(lhs[n, :, :WIDTH], rhs[rows, :], preferred_element_type=jnp.float32)
 
     def ctable(b, devs):
         return [send(ctabs.at[pl.ds(b, 1)], ctabs.at[pl.ds(b, 1)], dev) for dev in devs]
@@ -322,24 +322,21 @@
     multiply(3, 1, 1)
     unpack_last(mine4, core, 0, unroll=True)
     multiply(4, 0, 0)
-    multiply_last(core, 0)
+    acc[...] = multiply_last(core, 0)
     drain(4)
     arrived(last)
     unpack_last(theirs4, 1 - core, 1, unroll=True)
-    multiply_last(1 - core, 1)
+    product = multiply_last(1 - core, 1)
 
     lane = lax.broadcasted_iota(jnp.int32, (1, WIDTH), 1)
     fetch[1].wait()
-
-    def square(i, total):
-        rows = pl.ds(pl.multiple_of(i * T, T), T)
+    part = jnp.zeros((8, WIDTH), jnp.float32)
+    for i in range(RT):
         keep = jnp.where(lane < T, kt[0, i], kt[1, i]).astype(jnp.float32)
-        v = acc[rows, :]
+        v = product[i * T : (i + 1) * T]
         v = v * v * keep
-        acc[rows, :] = v
-        return total + jnp.sum(v.reshape(T // 8, 8, WIDTH), axis=0)
-
-    part = lax.fori_loop(0, RT, square, jnp.zeros((8, WIDTH), jnp.float32), unroll=True)
+        acc[i * T : (i + 1) * T] = v
+        part = part + jnp.sum(v.reshape(T // 8, 8, WIDTH), axis=0)
     cs[me_row] = jnp.sum(part, axis=0, keepdims=True)
     sums = [send(cs.at[me_row], cs.at[me_row], dev) for dev in peers]
     drain(len(sums))

time: 52 us -> 52 us (level)
  no operation moved by 1% of the time
where the time goes in v7:
time: 52 us; the launch traced here: 51.9 us
  Pallas kernels  50.4 us (97%)
  local copies, waits for them, and re-layouts  1.49 us (3%)
    pallas_call x1, Pallas kernels, body(): pl.pallas_call(kernel, out_shape=jax.ShapeDtypeStruct(markov.shape, jnp.b...  50.4 us
    unnamed x5, local copies, waits for them, and re-layouts  1.49 us

profile of v7, /device:TPU:1, one launch (start us, length us, event | category | flops | bytes accessed | tf_op | source)
XLA Modules:
  0.0 51.9 jit_solution(15576222394995680034)
XLA Ops:
  0.0 0.0 copy-start.1
  0.0 0.0 copy-start
  0.0 0.7 %copy-done.1 = s32[8,2]{0,1:T(2,128)S(1)} copy-done((s32[8,2]{0,1:T(2,128)S(1)}, s32[8,2]{0,1:T(2,128)}, u32[]{:S(2)}) %copy-start.1) | copy-done | bytes 88
  0.7 0.0 copy-done
  0.7 50.4 %cluster_step.1 = bf16[1024,256]{1,0:T(8,128)(2,1)S(1)} custom-call(bf16[8,128,256]{2,1,0:T(8,128)(2,1)} %bitcast.5, s32[2,8]{1,0:T(2,128)S(1)} %bitcast.3, s32[2,8]{1,0:T(2,128)S(1)} %bitcast.4), custom_call_target="tpu_custom_call" | custom-call | tf_op jit(solution)/shard_map/cluster_step/pallas_call | solution.py:364
  51.1 0.8 %copy.5 = bf16[1024,256]{1,0:T(8,128)(2,1)} copy(bf16[1024,256]{1,0:T(8,128)(2,1)S(1)} %cluster_step.1) | data formatting | bytes 1048576
Async XLA Ops:
  0.0 0.7 %copy-start.1 = (s32[8,2]{0,1:T(2,128)S(1)}, s32[8,2]{0,1:T(2,128)}, u32[]{:S(2)}) copy-start(s32[8,2]{0,1:T(2,128)} %param.5) | copy-start | bytes 196
  0.0 0.7 %copy-start = (s32[8,2]{0,1:T(2,128)S(1)}, s32[8,2]{0,1:T(2,128)}, u32[]{:S(2)}) copy-start(s32[8,2]{0,1:T(2,128)} %param.4) | copy-start | bytes 196
